TPU v7x, 32 devices: a whole 2x2x4 slice. The times are simulated.
32 devices in a mesh: expert: 4 (over z), dp: 8 (over y, x, core).
Axes of the slice: x: 2, y: 2, z: 4, core: 2. Of those that a mesh axis runs over, the one named last changes fastest.
Arguments:
- tokens: bfloat16 [1024, 4096], P(('dp', 'expert')), parts along dimension 0, may hold values from -6 to 6
- expert_ids: int32 [1024, 8], P(('dp', 'expert')), parts along dimension 0, may hold values from 0 to 127, as said below
- gates: bfloat16 [1024, 8], P(('dp', 'expert')), parts along dimension 0, may hold values from 0.099609375 to 1
- weights_in: bfloat16 [4, 4096, 768], P('expert'), may hold values from -0.09375 to 0.09375
- weights_out: bfloat16 [4, 384, 4096], P('expert'), may hold values from -0.21875 to 0.21875
Outputs:
- mixed: bfloat16 [1024, 4096], P(('dp', 'expert')), parts along dimension 0
There are 8 independent parts, one for each index of `dp`. A program takes and returns all parts, laid end to end along the dimension named above; an argument that names none is the same for every part. Nothing has to cross between parts.
Inputs may be any that keep to these rules, and one draw needn't show every extreme that they name: `expert_ids`: each row names 8 different experts. Of one device's 32 rows, each expert of 0 to 1 is named by at most 8 rows; one such expert is named by exactly 8 rows of every device, the others by at most 4 rows of each device and at least one.
All inputs are finite; a program needn't handle non-finite values.
Results may differ from a plain program's by a relative error of at most 0.0095.
Values may be sent and summed in bfloat16 or wider, within the bound.
A program may use at most 64 MiB of HBM per device.

v0:
```python
from functools import partial

import jax
import jax.numpy as jnp
from jax import lax
from jax.sharding import PartitionSpec as P

SRC_CAP = 8


def route_weights(expert_ids, gates, flight):
    expert_range = jnp.arange(flight, dtype=jnp.int32)
    matches = expert_ids[:, :, None] == expert_range[None, None, :]
    return jnp.sum(jnp.where(matches, gates[:, :, None], jnp.zeros((), gates.dtype)), axis=1)


def pick_slots(routed, capacity):
    position = jnp.cumsum(routed.astype(jnp.int32)) - 1
    slot_ids = jnp.arange(capacity, dtype=jnp.int32)
    matches = (position[None, :] == slot_ids[:, None]) & routed[None, :]
    row_ids = jnp.arange(routed.shape[0], dtype=jnp.int32)
    token_index = jnp.sum(matches.astype(jnp.int32) * row_ids[None, :], axis=1)
    filled = jnp.any(matches, axis=1)
    return (token_index, filled)


def expert_rows(picked, slot_gate, weights_in, weights_out):
    hidden_units = weights_out.shape[0]
    merged = jnp.dot(picked, weights_in, preferred_element_type=jnp.float32)
    hidden = (jax.nn.silu(merged[:, :hidden_units]) * merged[:, hidden_units:]).astype(jnp.bfloat16)
    output = jnp.dot(hidden, weights_out, preferred_element_type=jnp.float32)
    return output * slot_gate.astype(jnp.float32)[:, None]


def body(tokens, expert_ids, gates, weights_in, weights_out):
    devices = lax.axis_size("expert")
    flight = devices // 2
    width = tokens.shape[1]
    local_tokens = tokens.shape[0]
    weight_table = route_weights(expert_ids, gates, flight)
    token_index, filled = jax.vmap(partial(pick_slots, capacity=SRC_CAP), in_axes=1)(
        weight_table > 0
    )
    picked = tokens[token_index]
    slot_gate = jnp.take_along_axis(weight_table.T, token_index, axis=1)
    slot_gate = jnp.where(filled, slot_gate, jnp.zeros((), slot_gate.dtype))
    send_rows = jnp.repeat(picked, 2, axis=0)
    send_gates = jnp.repeat(slot_gate, 2, axis=0)
    rows_in = lax.all_to_all(send_rows, "expert", split_axis=0, concat_axis=0, tiled=True)
    gates_in = lax.all_to_all(send_gates, "expert", split_axis=0, concat_axis=0, tiled=True)
    flat_rows = rows_in.reshape(-1, width)
    output = expert_rows(flat_rows, gates_in.reshape(-1), weights_in[0], weights_out[0])
    output = output.astype(jnp.bfloat16).reshape(rows_in.shape)
    returned = lax.all_to_all(output, "expert", split_axis=0, concat_axis=0, tiled=True)
    pair_sum = jnp.sum(returned.astype(jnp.float32).reshape(flight, 2, SRC_CAP, width), axis=1)
    total = (
        jnp.zeros((local_tokens, width), jnp.float32)
        .at[token_index.reshape(-1)]
        .add(pair_sum.reshape(-1, width))
    )
    return total.astype(jnp.bfloat16)


def solution(mesh):
    return jax.shard_map(
        body,
        mesh=mesh,
        in_specs=(
            P(("dp", "expert"), None),
            P(("dp", "expert"), None),
            P(("dp", "expert"), None),
            P("expert", None, None),
            P("expert", None, None),
        ),
        out_specs=P(("dp", "expert"), None),
        check_vma=False,
    )
```

profile of v0, /device:TPU:0, one launch (start us, length us, event | category | flops | bytes accessed | tf_op | source)
XLA Modules:
  0.0 46.8 jit_solution(18203889161187376804)
XLA Ops:
  0.0 0.0 copy-start
  0.0 0.9 %fusion.15 = bf16[32,2]{0,1:T(2,128)(2,1)S(1)} fusion(s32[32,8]{0,1:T(8,128)} %param.6, bf16[32,8]{0,1:T(8,128)(2,1)} %param.7), kind=kLoop, calls=%fused_computation.24 | loop fusion | flops 1472 | bytes 1664 | tf_op jit(solution)/shard_map/reduce_sum | solution.py:14
  0.9 0.1 copy.28
  1.0 0.1 reduce_window_sum.11
  1.0 0.1 copy.29
  1.1 0.2 fusion.14
  1.3 0.2 select_reduce_fusion
  1.4 0.1 reshape.104
  1.5 0.7 %gather_fusion.1 = bf16[16]{0:T(256)(128)(2,1)S(1)} fusion(bf16[2,32]{1,0:T(2,128)(2,1)S(1)} %bitcast.34, s32[16]{0:T(128)S(1)} %reshape.104), kind=kCustom, calls=%fused_computation.1 | custom fusion | bytes 192 | tf_op jit(solution)/shard_map/jit(take_along_axis)/gather | solution.py:45
  2.2 0.1 reshape.107
  2.3 0.6 %copy.30 = bf16[4,1,8]{2,1,0:T(2,128)(2,1)} copy(bf16[4,1,8]{2,0,1:T(4,128)(2,1)S(1)} %bitcast.37) | data formatting | bytes 128 | tf_op jit(solution)/shard_map/all_to_all | solution.py:50
  2.9 6.3 %all-to-all-start.1 = ((bf16[4,1,8]{2,1,0:T(2,128)(2,1)}), bf16[4,1,8]{2,1,0:T(2,128)(2,1)S(1)}, u32[]{:S(2)}, u32[]{:S(2)}) async-start(bf16[4,1,8]{2,1,0:T(2,128)(2,1)} %copy.30), calls=%async_computation.1 | async-start | bytes 4096 | tf_op jit(solution)/shard_map/all_to_all | solution.py:50
  9.2 0.1 reshape.98
  9.3 1.7 %gather_fusion = bf16[16,4096]{1,0:T(8,128)(2,1)S(1)} fusion(bf16[32,4096]{1,0:T(8,128)(2,1)} %param.5, s32[1024]{0:T(1024)S(1)} %pad_clamp_fusion), kind=kCustom, calls=%fused_computation | custom fusion | bytes 262208 | tf_op jit(solution)/shard_map/gather | solution.py:44
  11.1 3.6 %all-to-all-done.1 = bf16[4,1,8]{2,1,0:T(2,128)(2,1)S(1)} async-done(((bf16[4,1,8]{2,1,0:T(2,128)(2,1)}), bf16[4,1,8]{2,1,0:T(2,128)(2,1)S(1)}, u32[]{:S(2)}, u32[]{:S(2)}) %all-to-all-start.1) | async-done | bytes 96 | tf_op jit(solution)/shard_map/all_to_all | solution.py:50
  14.7 0.7 %broadcast_in_dim.38 = bf16[2,2,8,4096]{3,2,1,0:T(8,128)(2,1)} broadcast(bf16[2,8,4096]{2,1,0:T(8,128)(2,1)S(1)} %bitcast.36), dimensions={0,2,3} | broadcast | bytes 393216 | tf_op jit(solution)/shard_map/broadcast_in_dim | solution.py:47
  15.4 3.4 %all-to-all-start = ((bf16[4,8,4096]{2,1,0:T(8,128)(2,1)}), bf16[4,8,4096]{2,1,0:T(8,128)(2,1)S(1)}, u32[]{:S(2)}, u32[]{:S(2)}) async-start(bf16[4,8,4096]{2,1,0:T(8,128)(2,1)} %bitcast.35), calls=%async_computation | async-start | bytes 524288 | tf_op jit(solution)/shard_map/all_to_all | solution.py:49
  18.9 0.1 reshape.93
  18.9 7.8 %all-to-all-done = bf16[4,8,4096]{2,1,0:T(8,128)(2,1)S(1)} async-done(((bf16[4,8,4096]{2,1,0:T(8,128)(2,1)}), bf16[4,8,4096]{2,1,0:T(8,128)(2,1)S(1)}, u32[]{:S(2)}, u32[]{:S(2)}) %all-to-all-start) | async-done | bytes 262176 | tf_op jit(solution)/shard_map/all_to_all | solution.py:49
  26.7 3.9 %fusion = f32[32,768]{1,0:T(8,128)S(1)} fusion(bf16[1,4096,768]{2,1,0:T(8,128)(2,1)} %param.8, bf16[4,8,4096]{2,1,0:T(8,128)(2,1)S(1)} %all-to-all-done), kind=kOutput, calls=%fused_computation.3 | convolution fusion | flops 201326592 | bytes 6651904 | tf_op jit(solution)/shard_map/dot_general | solution.py:29
  30.6 0.0 copy-done
  30.6 1.4 %fusion.3 = bf16[4,8,4096]{2,1,0:T(8,128)(2,1)} fusion(bf16[1,384,4096]{2,1,0:T(8,128)(2,1)S(1)} %copy-done, f32[32]{0:T(128)S(1)} %reshape.93, f32[32,768]{1,0:T(8,128)S(1)} %fusion), kind=kOutput, calls=%fused_computation.7 | convolution fusion | flops 100999168 | bytes 3506304 | tf_op jit(solution)/shard_map/dot_general | solution.py:31
  32.0 3.4 %all-to-all-start.2 = ((bf16[4,8,4096]{2,1,0:T(8,128)(2,1)}), bf16[4,8,4096]{2,1,0:T(8,128)(2,1)S(1)}, u32[]{:S(2)}, u32[]{:S(2)}) async-start(bf16[4,8,4096]{2,1,0:T(8,128)(2,1)} %fusion.3), calls=%async_computation.2 | async-start | bytes 524288 | tf_op jit(solution)/shard_map/all_to_all | solution.py:54
  35.4 0.1 reshape.86
  35.5 6.7 %all-to-all-done.2 = bf16[4,8,4096]{2,1,0:T(8,128)(2,1)S(1)} async-done(((bf16[4,8,4096]{2,1,0:T(8,128)(2,1)}), bf16[4,8,4096]{2,1,0:T(8,128)(2,1)S(1)}, u32[]{:S(2)}, u32[]{:S(2)}) %all-to-all-start.2) | async-done | bytes 262176 | tf_op jit(solution)/shard_map/all_to_all | solution.py:54
  42.2 0.7 %convert_reduce_fusion = f32[2,8,4096]{2,1,0:T(8,128)} fusion(bf16[4,8,4096]{2,1,0:T(8,128)(2,1)S(1)} %all-to-all-done.2), kind=kLoop, calls=%fused_computation.9 | loop fusion | flops 196608 | bytes 524288 | tf_op jit(solution)/shard_map/reduce_sum | solution.py:55
  42.9 2.1 %scatter_custom_fusion = f32[32,4096]{1,0:T(8,128)} fusion(s32[16]{0:T(128)S(1)} %fusion.16, f32[2,8,4096]{2,1,0:T(8,128)} %convert_reduce_fusion, f32[]{:T(128)} %constant.13.clone.1), kind=kCustom, calls=%fused_computation.10 | custom fusion | flops 65536 | bytes 786436 | tf_op jit(solution)/shard_map/scatter-add | solution.py:59
  45.0 1.8 %convert_element_type.31 = bf16[32,4096]{1,0:T(8,128)(2,1)} convert(f32[32,4096]{1,0:T(8,128)} %scatter_custom_fusion) | non-fusion elementwise | flops 131072 | bytes 786432 | tf_op jit(solution)/shard_map/convert_element_type | solution.py:61
  (9 shorter events, 0.1 us)
Async XLA Ops:
  0.0 30.6 %copy-start = (bf16[1,384,4096]{2,1,0:T(8,128)(2,1)S(1)}, bf16[1,384,4096]{2,1,0:T(8,128)(2,1)}, u32[]{:S(2)}) copy-start(bf16[1,384,4096]{2,1,0:T(8,128)(2,1)} %param.9) | copy-start | bytes 9437188
  2.9 11.8 %all-to-all-start.1 = ((bf16[4,1,8]{2,1,0:T(2,128)(2,1)}), bf16[4,1,8]{2,1,0:T(2,128)(2,1)S(1)}, u32[]{:S(2)}, u32[]{:S(2)}) async-start(bf16[4,1,8]{2,1,0:T(2,128)(2,1)} %copy.30), calls=%async_computation.1 | async-start | bytes 4096 | tf_op jit(solution)/shard_map/all_to_all | solution.py:50
  15.4 11.3 %all-to-all-start = ((bf16[4,8,4096]{2,1,0:T(8,128)(2,1)}), bf16[4,8,4096]{2,1,0:T(8,128)(2,1)S(1)}, u32[]{:S(2)}, u32[]{:S(2)}) async-start(bf16[4,8,4096]{2,1,0:T(8,128)(2,1)} %bitcast.35), calls=%async_computation | async-start | bytes 524288 | tf_op jit(solution)/shard_map/all_to_all | solution.py:49
  32.0 10.2 %all-to-all-start.2 = ((bf16[4,8,4096]{2,1,0:T(8,128)(2,1)}), bf16[4,8,4096]{2,1,0:T(8,128)(2,1)S(1)}, u32[]{:S(2)}, u32[]{:S(2)}) async-start(bf16[4,8,4096]{2,1,0:T(8,128)(2,1)} %fusion.3), calls=%async_computation.2 | async-start | bytes 524288 | tf_op jit(solution)/shard_map/all_to_all | solution.py:54
where the time goes:
time: 47.3 us; the launch traced here: 46.8 us
  waiting for transfers between devices  18.1 us (38%)
  starting transfers between devices  13.1 us (28%)
  other arithmetic  5.93 us (13%)
  matrix products  5.28 us (11%)
  local copies, waits for them, and re-layouts  4.32 us (9%)
    all_to_all x1, waiting for transfers between devices, body(): lax.all_to_all(send_rows, 'expert', split_axis=0, concat_axis=0, tiled=True)  7.78 us
    all_to_all x1, waiting for transfers between devices, body(): lax.all_to_all(output, 'expert', split_axis=0, concat_axis=0, tiled=True)  6.65 us
    all_to_all x1, starting transfers between devices, body(): lax.all_to_all(send_gates, 'expert', split_axis=0, concat_axis=0, tiled=T...  6.32 us
    dot_general x1, matrix products, expert_rows(): merged = jnp.dot(picked, weights_in, preferred_element_type=jnp.float32)  3.9 us
    all_to_all x1, waiting for transfers between devices, body(): lax.all_to_all(send_gates, 'expert', split_axis=0, concat_axis=0, tiled=T...  3.64 us
    all_to_all x1, starting transfers between devices, body(): lax.all_to_all(send_rows, 'expert', split_axis=0, concat_axis=0, tiled=True)  3.41 us
    all_to_all x1, starting transfers between devices, body(): lax.all_to_all(output, 'expert', split_axis=0, concat_axis=0, tiled=True)  3.41 us
    scatter-add x1, other arithmetic, body(): total = jnp.zeros((local_tokens, width), jnp.float32).at[token_index.resh...  2.12 us
  transfers between devices with their start and end apart: 3, of which 3 were waited for; matrix products, arithmetic and copies ran while one was open for 4% of the time, Pallas kernels for 0%

commit v1 on v0

v1 whole, which is shorter than its diff:
```python
from functools import partial

import jax
import jax.numpy as jnp
from jax import lax
from jax.experimental import pallas as pl
from jax.experimental.pallas import tpu as pltpu
from jax.sharding import PartitionSpec as P

SRC_CAP = 8
PACK = 2 * SRC_CAP
IN_CHUNKS = 4
OUT_CHUNKS = 4
MESH = pl.DeviceIdType.MESH


def slot_matrix(value, routed, position, rows, rows_per_expert):
    tokens = value[0].shape[1]
    row = lax.broadcasted_iota(jnp.int32, (rows, tokens), 0)
    slot = (row % SRC_CAP).astype(jnp.float32)
    expert = row // rows_per_expert
    table = jnp.zeros((rows, tokens), jnp.float32)
    for e in range(len(value)):
        hit = (expert == e) & (position[e] == slot) & (routed[e] > 0.0)
        table = jnp.where(hit, value[e], table)
    return table


def split_halves(table, axis):
    half = (lax.broadcasted_iota(jnp.int32, table.shape, axis) // SRC_CAP) % 2
    zero = jnp.zeros_like(table)
    return jnp.where(half == 0, table, zero), jnp.where(half == 1, table, zero)


def kernel(
    n,
    tok_hbm,
    ids_hbm,
    gate_hbm,
    win_hbm,
    wout_hbm,
    out_ref,
    tok,
    ids,
    gate,
    win,
    wout,
    send_rows,
    recv_rows,
    send_out,
    recv_out,
    small_sem,
    win_sem,
    wout_sem,
    row_send_sem,
    row_recv_sem,
    out_send_sem,
    out_recv_sem,
):
    me = lax.axis_index("expert")
    flight = n // 2
    width = tok.shape[1]
    hid = wout.shape[0]
    in_width = width // IN_CHUNKS
    in_half = in_width // 2
    out_width = width // OUT_CHUNKS
    out_half = out_width // 2

    def peer(d):
        return lax.rem(me + d, n)

    barrier = pltpu.get_barrier_semaphore()
    for d in range(1, n):
        pl.semaphore_signal(barrier, inc=1, device_id={"expert": peer(d)}, device_id_type=MESH)

    small = [
        pltpu.make_async_copy(ids_hbm, ids, small_sem.at[0]),
        pltpu.make_async_copy(gate_hbm, gate, small_sem.at[1]),
        pltpu.make_async_copy(tok_hbm, tok, small_sem.at[2]),
    ]
    for copy in small:
        copy.start()

    def win_copy(c):
        rows = pl.ds(c * in_width, in_width)
        return pltpu.make_async_copy(win_hbm.at[0, rows], win.at[rows], win_sem.at[c])

    wout_copy = pltpu.make_async_copy(wout_hbm.at[0], wout, wout_sem)
    for c in range(IN_CHUNKS):
        win_copy(c).start()
    wout_copy.start()

    small[0].wait()
    small[1].wait()
    chosen = ids[...]
    gates = gate[...].astype(jnp.float32)
    tokens = chosen.shape[1]
    weight, routed = [], []
    for e in range(flight):
        match = chosen == e
        weight.append(jnp.sum(jnp.where(match, gates, 0.0), axis=0, keepdims=True))
        routed.append(jnp.sum(jnp.where(match, 1.0, 0.0), axis=0, keepdims=True))
    row = lax.broadcasted_iota(jnp.int32, (PACK, tokens), 0)
    marks = jnp.zeros((PACK, tokens), jnp.float32)
    for e in range(flight):
        marks = jnp.where(row == e, routed[e], marks)
    before = lax.broadcasted_iota(jnp.int32, (tokens, tokens), 0) < lax.broadcasted_iota(
        jnp.int32, (tokens, tokens), 1
    )
    ahead = jnp.dot(
        marks.astype(jnp.bfloat16),
        before.astype(jnp.float32).astype(jnp.bfloat16),
        preferred_element_type=jnp.float32,
    )
    position = [ahead[e : e + 1] for e in range(flight)]
    pick = slot_matrix(routed, routed, position, flight * PACK, PACK)
    pick = [part.astype(jnp.bfloat16) for part in split_halves(pick, 0)]

    def row_copy(d, c):
        dst = peer(d)
        return pltpu.make_async_remote_copy(
            src_ref=send_rows.at[dst // 2, c],
            dst_ref=recv_rows.at[me, c],
            send_sem=row_send_sem.at[dst, c],
            recv_sem=row_recv_sem.at[me, c],
            device_id={"expert": dst},
            device_id_type=MESH,
        )

    def row_arrival(d, c):
        src = peer(d)
        return pltpu.make_async_remote_copy(
            src_ref=send_rows.at[0, c],
            dst_ref=recv_rows.at[src, c],
            send_sem=row_send_sem.at[src, c],
            recv_sem=row_recv_sem.at[src, c],
            device_id={"expert": src},
            device_id_type=MESH,
        )

    small[2].wait()
    for c in range(IN_CHUNKS):
        lo = c * in_width
        rows = sum(
            jnp.dot(
                pick[half],
                tok[:, lo + half * in_half : lo + (half + 1) * in_half],
                preferred_element_type=jnp.float32,
            )
            for half in range(2)
        ).astype(jnp.bfloat16)
        send_rows[:, c] = rows.reshape(flight, PACK, in_half)
        if c == 0:
            pl.semaphore_wait(barrier, n - 1)
        for d in range(1, n):
            row_copy(d, c).start()
        recv_rows[me, c] = send_rows[me // 2, c]

    combine = jnp.transpose(slot_matrix(weight, routed, position, n * PACK, 2 * PACK))
    combine = jnp.concatenate(split_halves(combine, 1), axis=0).astype(jnp.bfloat16)

    def in_step(c, total):
        win_copy(c).wait()
        for d in range(1, n):
            row_arrival(d, c).wait_recv()
        packed = recv_rows[:, c].astype(jnp.float32)
        for half in range(2):
            rows = packed[:, half * SRC_CAP : (half + 1) * SRC_CAP].reshape(n * SRC_CAP, in_half)
            start = pl.multiple_of(c * in_width + half * in_half, in_half)
            total = total + jnp.dot(
                rows.astype(jnp.bfloat16),
                win[pl.ds(start, in_half)],
                preferred_element_type=jnp.float32,
            )
        return total

    merged = lax.fori_loop(
        0, IN_CHUNKS, in_step, jnp.zeros((n * SRC_CAP, 2 * hid), jnp.float32)
    )
    left = merged[:, :hid]
    hidden = (left / (1.0 + jnp.exp(-left)) * merged[:, hid:]).astype(jnp.bfloat16)

    def out_copy(d, c):
        dst = peer(d)
        return pltpu.make_async_remote_copy(
            src_ref=send_out.at[dst, c],
            dst_ref=recv_out.at[me, c],
            send_sem=out_send_sem.at[dst, c],
            recv_sem=out_recv_sem.at[me, c],
            device_id={"expert": dst},
            device_id_type=MESH,
        )

    def out_arrival(d, c):
        src = peer(d)
        return pltpu.make_async_remote_copy(
            src_ref=send_out.at[src, c],
            dst_ref=recv_out.at[src, c],
            send_sem=out_send_sem.at[src, c],
            recv_sem=out_recv_sem.at[src, c],
            device_id={"expert": src},
            device_id_type=MESH,
        )

    wout_copy.wait()
    for c in range(OUT_CHUNKS):
        lo = c * out_width
        output = jnp.dot(
            hidden, wout[:, lo : lo + out_width], preferred_element_type=jnp.float32
        ).reshape(n, SRC_CAP, out_width)
        packed = jnp.concatenate([output[:, :, :out_half], output[:, :, out_half:]], axis=1)
        send_out[:, c] = packed.astype(jnp.bfloat16)
        for d in range(1, n):
            out_copy(d, c).start()
        recv_out[me, c] = send_out[me, c]

    for c in range(OUT_CHUNKS):
        lo = c * out_width
        for d in range(1, n):
            out_arrival(d, c).wait_recv()
        packed = recv_out[:, c].reshape(n * PACK, out_half)
        mixed = jnp.dot(combine, packed, preferred_element_type=jnp.float32).astype(jnp.bfloat16)
        out_ref[:, lo : lo + out_half] = mixed[:tokens]
        out_ref[:, lo + out_half : lo + out_width] = mixed[tokens:]

    for c in range(IN_CHUNKS):
        for d in range(1, n):
            row_copy(d, c).wait_send()
    for c in range(OUT_CHUNKS):
        for d in range(1, n):
            out_copy(d, c).wait_send()


def body(tokens, expert_ids, gates, weights_in, weights_out):
    n = lax.axis_size("expert")
    flight = n // 2
    local, width = tokens.shape
    hid = weights_out.shape[1]
    in_half = width // IN_CHUNKS // 2
    out_half = width // OUT_CHUNKS // 2
    dtype = tokens.dtype
    return pl.pallas_call(
        partial(kernel, n),
        out_shape=jax.ShapeDtypeStruct((local, width), dtype),
        in_specs=[pl.BlockSpec(memory_space=pl.ANY)] * 5,
        out_specs=pl.BlockSpec(memory_space=pltpu.VMEM),
        scratch_shapes=[
            pltpu.VMEM((local, width), dtype),
            pltpu.VMEM(expert_ids.shape[::-1], expert_ids.dtype),
            pltpu.VMEM(gates.shape[::-1], gates.dtype),
            pltpu.VMEM(weights_in.shape[1:], weights_in.dtype),
            pltpu.VMEM(weights_out.shape[1:], weights_out.dtype),
            pltpu.VMEM((flight, IN_CHUNKS, PACK, in_half), dtype),
            pltpu.VMEM((n, IN_CHUNKS, PACK, in_half), dtype),
            pltpu.VMEM((n, OUT_CHUNKS, PACK, out_half), dtype),
            pltpu.VMEM((n, OUT_CHUNKS, PACK, out_half), dtype),
            pltpu.SemaphoreType.DMA((3,)),
            pltpu.SemaphoreType.DMA((IN_CHUNKS,)),
            pltpu.SemaphoreType.DMA,
            pltpu.SemaphoreType.DMA((n, IN_CHUNKS)),
            pltpu.SemaphoreType.DMA((n, IN_CHUNKS)),
            pltpu.SemaphoreType.DMA((n, OUT_CHUNKS)),
            pltpu.SemaphoreType.DMA((n, OUT_CHUNKS)),
        ],
        compiler_params=pltpu.CompilerParams(
            collective_id=0, has_side_effects=True, vmem_limit_bytes=62 * 2**20
        ),
    )(tokens, expert_ids.T, gates.T, weights_in, weights_out)


def solution(mesh):
    return jax.shard_map(
        body,
        mesh=mesh,
        in_specs=(
            P(("dp", "expert"), None),
            P(("dp", "expert"), None),
            P(("dp", "expert"), None),
            P("expert", None, None),
            P("expert", None, None),
        ),
        out_specs=P(("dp", "expert"), None),
        check_vma=False,
    )
```

time: 47.3 us -> 22.6 us (0.48)
  Pallas kernels: 0 us -> 20.8 us
  waiting for transfers between devices: 18.1 us -> 0 us
  starting transfers between devices: 13.1 us -> 0 us
  other arithmetic: 5.93 us -> 0 us
  matrix products: 5.28 us -> 0 us
  local copies, waits for them, and re-layouts: 4.32 us -> 1.67 us
    pallas_call x0 -> x1, Pallas kernels: none -> 20.8 us  [body(): pl.pallas_call(partial(kernel, n), out_shape=jax.ShapeDtypeStruct((local,...]
    all_to_all x3 -> x0, waiting for transfers between devices: 18.1 us -> none  [the longest x1 7.78 us: body(): lax.all_to_all(send_rows, 'expert', split_axis=0, concat_axis=0, tiled=True)]
    all_to_all x3 -> x0, starting transfers between devices: 13.1 us -> none  [the longest x1 6.32 us: body(): lax.all_to_all(send_gates, 'expert', split_axis=0, concat_axis=0, tiled=T...]
    dot_general x2 -> x0, matrix products: 5.28 us -> none  [the longest x1 3.9 us: expert_rows(): merged = jnp.dot(picked, weights_in, preferred_element_type=jnp.float32)]
    gather x4 -> x0, local copies, waits for them, and re-layouts: 2.58 us -> none  [the longest x1 1.73 us: body(): picked = tokens[token_index]]
    scatter-add x1 -> x0, other arithmetic: 2.12 us -> none  [body(): total = jnp.zeros((local_tokens, width), jnp.float32).at[token_index.resh...]
    convert_element_type x3 -> x0, other arithmetic: 1.79 us -> none  [the longest x1 1.77 us: body(): return total.astype(jnp.bfloat16)]
    reduce_sum x3 -> x0, other arithmetic: 1.75 us -> none  [the longest x1 0.87 us: route_weights(): jnp.sum(jnp.where(matches, gates[:, :, None], jnp.zeros((), gates.dtype))...]
  transfers between devices with their start and end apart: 3 -> 0, of which waited for: 3 -> 0; matrix products, arithmetic and copies ran while one was open for 4% -> 0% of each run, Pallas kernels for 0% -> 0%
where the time goes in v1:
time: 22.6 us; the launch traced here: 22.5 us
  Pallas kernels  20.8 us (92%)
  local copies, waits for them, and re-layouts  1.67 us (7%)
    pallas_call x1, Pallas kernels, body(): pl.pallas_call(partial(kernel, n), out_shape=jax.ShapeDtypeStruct((local,...  20.8 us
    unnamed x1, local copies, waits for them, and re-layouts  1.67 us

profile of v1, /device:TPU:0, one launch (start us, length us, event | category | flops | bytes accessed | tf_op | source)
XLA Modules:
  0.0 22.5 jit_solution(12150214725957709857)
XLA Ops:
  0.0 20.8 %shard_map.55 = bf16[32,4096]{1,0:T(8,128)(2,1)} custom-call(bf16[32,4096]{1,0:T(8,128)(2,1)} %tok_hbm.1, s32[8,32]{1,0:T(8,128)} %bitcast.2, bf16[8,32]{1,0:T(8,128)(2,1)} %bitcast.3, bf16[1,4096,768]{2,1,0:T(8,128)(2,1)} %win_hbm.1, bf16[1,384,4096]{2,1,0:T(8,128)(2,1)} %wout_hbm.1), custom_call_target="tpu_custom_call" | custom-call | tf_op jit(solution)/shard_map/pallas_call | solution.py:242
  20.8 1.7 %copy.7 = bf16[32,4096]{1,0:T(8,128)(2,1)} copy(bf16[32,4096]{1,0:T(8,128)(2,1)} %shard_map.55) | data formatting | bytes 524288

commit v2 on v1

--- a/solution.py
+++ b/solution.py
@@ -241,8 +241,8 @@
     dtype = tokens.dtype
     return pl.pallas_call(
         partial(kernel, n),
-        out_shape=jax.ShapeDtypeStruct((local, width), dtype),
-        in_specs=[pl.BlockSpec(memory_space=pl.ANY)] * 5,
+        out_shape=pltpu.VMEM((local, width), dtype),
+        in_specs=[pl.BlockSpec(memory_space=pltpu.HBM)] * 5,
         out_specs=pl.BlockSpec(memory_space=pltpu.VMEM),
         scratch_shapes=[
             pltpu.VMEM((local, width), dtype),
@@ -263,7 +263,7 @@
             pltpu.SemaphoreType.DMA((n, OUT_CHUNKS)),
         ],
         compiler_params=pltpu.CompilerParams(
-            collective_id=0, has_side_effects=True, vmem_limit_bytes=62 * 2**20
+            collective_id=0, has_side_effects=True, vmem_limit_bytes=56 * 2**20
         ),
     )(tokens, expert_ids.T, gates.T, weights_in, weights_out)
 

time: 22.6 us -> 21 us (0.929)
  local copies, waits for them, and re-layouts: 1.67 us -> 0.71 us
  Pallas kernels: 20.8 us -> 20.1 us
    unnamed x1, local copies, waits for them, and re-layouts: 1.67 us -> 0.71 us
    pallas_call x1, Pallas kernels: 20.8 us -> 20.1 us  [body(): pl.pallas_call(partial(kernel, n), out_shape=pltpu.VMEM((local, width), d...]
where the time goes in v2:
time: 21 us; the launch traced here: 20.8 us
  Pallas kernels  20.1 us (96%)
  local copies, waits for them, and re-layouts  0.71 us (3%)
    pallas_call x1, Pallas kernels, body(): pl.pallas_call(partial(kernel, n), out_shape=pltpu.VMEM((local, width), d...  20.1 us
    unnamed x1, local copies, waits for them, and re-layouts  0.71 us

profile of v2, /device:TPU:0, one launch (start us, length us, event | category | flops | bytes accessed | tf_op | source)
XLA Modules:
  0.0 20.8 jit_solution(1175791921951539954)
XLA Ops:
  0.0 20.1 %shard_map.55 = bf16[32,4096]{1,0:T(8,128)(2,1)S(1)} custom-call(bf16[32,4096]{1,0:T(8,128)(2,1)} %tok_hbm.1, s32[8,32]{1,0:T(8,128)} %bitcast.2, bf16[8,32]{1,0:T(8,128)(2,1)} %bitcast.3, bf16[1,4096,768]{2,1,0:T(8,128)(2,1)} %win_hbm.1, bf16[1,384,4096]{2,1,0:T(8,128)(2,1)} %wout_hbm.1), custom_call_target="tpu_custom_call" | custom-call | tf_op jit(solution)/shard_map/pallas_call | solution.py:242
  20.1 0.7 %copy.7 = bf16[32,4096]{1,0:T(8,128)(2,1)} copy(bf16[32,4096]{1,0:T(8,128)(2,1)S(1)} %shard_map.55) | data formatting | bytes 524288

commit v3 on v2

--- a/solution.py
+++ b/solution.py
@@ -11,6 +11,8 @@
 PACK = 2 * SRC_CAP
 IN_CHUNKS = 4
 OUT_CHUNKS = 4
+RELAY_IN = 2
+RELAY_OUT = 2
 MESH = pl.DeviceIdType.MESH
 
 
@@ -49,6 +51,7 @@
     recv_rows,
     send_out,
     recv_out,
+    partial_out,
     small_sem,
     win_sem,
     wout_sem,
@@ -56,6 +59,8 @@
     row_recv_sem,
     out_send_sem,
     out_recv_sem,
+    relay_sem,
+    partial_sem,
 ):
     me = lax.axis_index("expert")
     flight = n // 2
@@ -66,8 +71,22 @@
     out_width = width // OUT_CHUNKS
     out_half = out_width // 2
 
+    pair = me // 2
+    partner = me + 1 - 2 * (me % 2)
+
     def peer(d):
         return lax.rem(me + d, n)
+
+    def other_pair(k):
+        return lax.rem(pair + k, flight)
+
+    def near_of(source, target_pair):
+        return 2 * target_pair + jnp.where(source < 2 * target_pair, 0, 1)
+
+    def others():
+        for k in range(1, flight):
+            for member in range(2):
+                yield 2 * other_pair(k) + member
 
     barrier = pltpu.get_barrier_semaphore()
     for d in range(1, n):
@@ -116,8 +135,7 @@
     pick = slot_matrix(routed, routed, position, flight * PACK, PACK)
     pick = [part.astype(jnp.bfloat16) for part in split_halves(pick, 0)]
 
-    def row_copy(d, c):
-        dst = peer(d)
+    def row_copy(dst, c):
         return pltpu.make_async_remote_copy(
             src_ref=send_rows.at[dst // 2, c],
             dst_ref=recv_rows.at[me, c],
@@ -127,16 +145,23 @@
             device_id_type=MESH,
         )
 
-    def row_arrival(d, c):
-        src = peer(d)
+    def relay_copy(src, c):
         return pltpu.make_async_remote_copy(
-            src_ref=send_rows.at[0, c],
+            src_ref=recv_rows.at[src, c],
             dst_ref=recv_rows.at[src, c],
-            send_sem=row_send_sem.at[src, c],
+            send_sem=relay_sem.at[src, c],
             recv_sem=row_recv_sem.at[src, c],
-            device_id={"expert": src},
+            device_id={"expert": partner},
             device_id_type=MESH,
         )
+
+    def row_targets(c):
+        for k in range(1, flight):
+            near = near_of(me, other_pair(k))
+            yield near
+            if c >= RELAY_IN:
+                yield 4 * other_pair(k) + 1 - near
+        yield partner
 
     small[2].wait()
     for c in range(IN_CHUNKS):
@@ -152,8 +177,8 @@
         send_rows[:, c] = rows.reshape(flight, PACK, in_half)
         if c == 0:
             pl.semaphore_wait(barrier, n - 1)
-        for d in range(1, n):
-            row_copy(d, c).start()
+        for dst in row_targets(c):
+            row_copy(dst, c).start()
         recv_rows[me, c] = send_rows[me // 2, c]
 
     combine = jnp.transpose(slot_matrix(weight, routed, position, n * PACK, 2 * PACK))
@@ -161,8 +186,14 @@
 
     def in_step(c, total):
         win_copy(c).wait()
-        for d in range(1, n):
-            row_arrival(d, c).wait_recv()
+        for src in others():
+            relay_copy(src, c).wait_recv()
+
+            @pl.when((near_of(src, pair) == me) & (c < RELAY_IN))
+            def _():
+                relay_copy(src, c).start()
+
+        relay_copy(partner, c).wait_recv()
         packed = recv_rows[:, c].astype(jnp.float32)
         for half in range(2):
             rows = packed[:, half * SRC_CAP : (half + 1) * SRC_CAP].reshape(n * SRC_CAP, in_half)
@@ -180,25 +211,23 @@
     left = merged[:, :hid]
     hidden = (left / (1.0 + jnp.exp(-left)) * merged[:, hid:]).astype(jnp.bfloat16)
 
-    def out_copy(d, c):
-        dst = peer(d)
+    def out_copy(dst, c, slot):
         return pltpu.make_async_remote_copy(
             src_ref=send_out.at[dst, c],
-            dst_ref=recv_out.at[me, c],
+            dst_ref=recv_out.at[slot, c],
             send_sem=out_send_sem.at[dst, c],
-            recv_sem=out_recv_sem.at[me, c],
+            recv_sem=out_recv_sem.at[slot, c],
             device_id={"expert": dst},
             device_id_type=MESH,
         )
 
-    def out_arrival(d, c):
-        src = peer(d)
+    def partial_copy(dst, c):
         return pltpu.make_async_remote_copy(
-            src_ref=send_out.at[src, c],
-            dst_ref=recv_out.at[src, c],
-            send_sem=out_send_sem.at[src, c],
-            recv_sem=out_recv_sem.at[src, c],
-            device_id={"expert": src},
+            src_ref=send_out.at[dst, c],
+            dst_ref=partial_out.at[dst, c],
+            send_sem=out_send_sem.at[dst, c],
+            recv_sem=partial_sem.at[dst, c],
+            device_id={"expert": partner},
             device_id_type=MESH,
         )
 
@@ -210,25 +239,58 @@
         ).reshape(n, SRC_CAP, out_width)
         packed = jnp.concatenate([output[:, :, :out_half], output[:, :, out_half:]], axis=1)
         send_out[:, c] = packed.astype(jnp.bfloat16)
-        for d in range(1, n):
-            out_copy(d, c).start()
+        for dst in others():
+            if c < RELAY_OUT:
+
+                @pl.when(near_of(dst, pair) != me)
+                def _():
+                    partial_copy(dst, c).start()
+            else:
+                out_copy(dst, c, me).start()
+        out_copy(partner, c, me).start()
         recv_out[me, c] = send_out[me, c]
 
-    for c in range(OUT_CHUNKS):
+    for c in range(RELAY_OUT):
+        for dst in others():
+
+            @pl.when(near_of(dst, pair) == me)
+            def _():
+                partial_copy(dst, c).wait_recv()
+                both = send_out[dst, c].astype(jnp.float32) + partial_out[dst, c].astype(
+                    jnp.float32
+                )
+                send_out[dst, c] = both.astype(jnp.bfloat16)
+                out_copy(dst, c, 2 * pair).start()
+
+        for k in range(1, flight):
+            recv_out[2 * other_pair(k) + 1, c] = jnp.zeros((PACK, out_half), recv_out.dtype)
+
+    for c in list(range(RELAY_OUT, OUT_CHUNKS)) + list(range(RELAY_OUT)):
         lo = c * out_width
-        for d in range(1, n):
-            out_arrival(d, c).wait_recv()
+        out_copy(partner, c, partner).wait_recv()
+        for k in range(1, flight):
+            out_copy(partner, c, 2 * other_pair(k)).wait_recv()
+            if c >= RELAY_OUT:
+                out_copy(partner, c, 2 * other_pair(k) + 1).wait_recv()
         packed = recv_out[:, c].reshape(n * PACK, out_half)
         mixed = jnp.dot(combine, packed, preferred_element_type=jnp.float32).astype(jnp.bfloat16)
         out_ref[:, lo : lo + out_half] = mixed[:tokens]
         out_ref[:, lo + out_half : lo + out_width] = mixed[tokens:]
 
     for c in range(IN_CHUNKS):
-        for d in range(1, n):
-            row_copy(d, c).wait_send()
+        for dst in row_targets(c):
+            row_copy(dst, c).wait_send()
+        if c < RELAY_IN:
+            for src in others():
+
+                @pl.when(near_of(src, pair) == me)
+                def _():
+                    relay_copy(src, c).wait_send()
+
     for c in range(OUT_CHUNKS):
-        for d in range(1, n):
-            out_copy(d, c).wait_send()
+        for dst in others():
+            out_copy(dst, c, me).wait_send()
+        out_copy(partner, c, me).wait_send()
 
 
 def body(tokens, expert_ids, gates, weights_in, weights_out):
@@ -254,12 +316,15 @@
             pltpu.VMEM((n, IN_CHUNKS, PACK, in_half), dtype),
             pltpu.VMEM((n, OUT_CHUNKS, PACK, out_half), dtype),
             pltpu.VMEM((n, OUT_CHUNKS, PACK, out_half), dtype),
+            pltpu.VMEM((n, max(RELAY_OUT, 1), PACK, out_half), dtype),
             pltpu.SemaphoreType.DMA((3,)),
             pltpu.SemaphoreType.DMA((IN_CHUNKS,)),
             pltpu.SemaphoreType.DMA,
             pltpu.SemaphoreType.DMA((n, IN_CHUNKS)),
             pltpu.SemaphoreType.DMA((n, IN_CHUNKS)),
             pltpu.SemaphoreType.DMA((n, OUT_CHUNKS)),
+            pltpu.SemaphoreType.DMA((n, OUT_CHUNKS)),
+            pltpu.SemaphoreType.DMA((n, IN_CHUNKS)),
             pltpu.SemaphoreType.DMA((n, OUT_CHUNKS)),
         ],
         compiler_params=pltpu.CompilerParams(

time: 21 us -> 22.1 us (1.052)
  Pallas kernels: 20.1 us -> 21.2 us
    pallas_call x1, Pallas kernels: 20.1 us -> 21.2 us  [body(): pl.pallas_call(partial(kernel, n), out_shape=pltpu.VMEM((local, width), d...]
where the time goes in v3:
time: 22.1 us; the launch traced here: 22 us
  Pallas kernels  21.2 us (96%)
  local copies, waits for them, and re-layouts  0.71 us (3%)
    pallas_call x1, Pallas kernels, body(): pl.pallas_call(partial(kernel, n), out_shape=pltpu.VMEM((local, width), d...  21.2 us
    unnamed x1, local copies, waits for them, and re-layouts  0.71 us

profile of v3, /device:TPU:0, one launch (start us, length us, event | category | flops | bytes accessed | tf_op | source)
XLA Modules:
  0.0 22.0 jit_solution(1802591506639345360)
XLA Ops:
  0.0 21.2 %shard_map.55 = bf16[32,4096]{1,0:T(8,128)(2,1)S(1)} custom-call(bf16[32,4096]{1,0:T(8,128)(2,1)} %tok_hbm.1, s32[8,32]{1,0:T(8,128)} %bitcast.2, bf16[8,32]{1,0:T(8,128)(2,1)} %bitcast.3, bf16[1,4096,768]{2,1,0:T(8,128)(2,1)} %win_hbm.1, bf16[1,384,4096]{2,1,0:T(8,128)(2,1)} %wout_hbm.1), custom_call_target="tpu_custom_call" | custom-call | tf_op jit(solution)/shard_map/pallas_call | solution.py:304
  21.3 0.7 %copy.7 = bf16[32,4096]{1,0:T(8,128)(2,1)} copy(bf16[32,4096]{1,0:T(8,128)(2,1)S(1)} %shard_map.55) | data formatting | bytes 524288

commit v4 on v3

--- a/solution.py
+++ b/solution.py
@@ -9,10 +9,10 @@
 
 SRC_CAP = 8
 PACK = 2 * SRC_CAP
-IN_CHUNKS = 4
-OUT_CHUNKS = 4
-RELAY_IN = 2
-RELAY_OUT = 2
+IN_CHUNKS = 2
+OUT_CHUNKS = 2
+RELAY_IN = 0
+RELAY_OUT = 0
 MESH = pl.DeviceIdType.MESH
 
 

time: 22.1 us -> 20.6 us (0.932)
  Pallas kernels: 21.2 us -> 19.7 us
    pallas_call x1, Pallas kernels: 21.2 us -> 19.7 us  [body(): pl.pallas_call(partial(kernel, n), out_shape=pltpu.VMEM((local, width), d...]
where the time goes in v4:
time: 20.6 us; the launch traced here: 20.4 us
  Pallas kernels  19.7 us (96%)
  local copies, waits for them, and re-layouts  0.71 us (3%)
    pallas_call x1, Pallas kernels, body(): pl.pallas_call(partial(kernel, n), out_shape=pltpu.VMEM((local, width), d...  19.7 us
    unnamed x1, local copies, waits for them, and re-layouts  0.71 us

profile of v4, /device:TPU:0, one launch (start us, length us, event | category | flops | bytes accessed | tf_op | source)
XLA Modules:
  0.0 20.4 jit_solution(13803217887706506990)
XLA Ops:
  0.0 19.7 %shard_map.55 = bf16[32,4096]{1,0:T(8,128)(2,1)S(1)} custom-call(bf16[32,4096]{1,0:T(8,128)(2,1)} %tok_hbm.1, s32[8,32]{1,0:T(8,128)} %bitcast.2, bf16[8,32]{1,0:T(8,128)(2,1)} %bitcast.3, bf16[1,4096,768]{2,1,0:T(8,128)(2,1)} %win_hbm.1, bf16[1,384,4096]{2,1,0:T(8,128)(2,1)} %wout_hbm.1), custom_call_target="tpu_custom_call" | custom-call | tf_op jit(solution)/shard_map/pallas_call | solution.py:304
  19.7 0.7 %copy.7 = bf16[32,4096]{1,0:T(8,128)(2,1)} copy(bf16[32,4096]{1,0:T(8,128)(2,1)S(1)} %shard_map.55) | data formatting | bytes 524288

commit v5 on v4

--- a/solution.py
+++ b/solution.py
@@ -9,7 +9,8 @@
 
 SRC_CAP = 8
 PACK = 2 * SRC_CAP
-IN_CHUNKS = 2
+IN_CHUNKS = 4
+IN_FLIGHT = 2
 OUT_CHUNKS = 2
 RELAY_IN = 0
 RELAY_OUT = 0
@@ -177,6 +178,9 @@
         send_rows[:, c] = rows.reshape(flight, PACK, in_half)
         if c == 0:
             pl.semaphore_wait(barrier, n - 1)
+        if c >= IN_FLIGHT:
+            for dst in row_targets(c - IN_FLIGHT):
+                row_copy(dst, c - IN_FLIGHT).wait_send()
         for dst in row_targets(c):
             row_copy(dst, c).start()
         recv_rows[me, c] = send_rows[me // 2, c]
@@ -278,8 +282,9 @@
         out_ref[:, lo + out_half : lo + out_width] = mixed[tokens:]
 
     for c in range(IN_CHUNKS):
-        for dst in row_targets(c):
-            row_copy(dst, c).wait_send()
+        if c >= IN_CHUNKS - IN_FLIGHT:
+            for dst in row_targets(c):
+                row_copy(dst, c).wait_send()
         if c < RELAY_IN:
             for src in others():
 

time: 20.6 us -> 20.6 us (level)
  no operation moved by 1% of the time
where the time goes in v5:
time: 20.6 us; the launch traced here: 20.5 us
  Pallas kernels  19.8 us (96%)
  local copies, waits for them, and re-layouts  0.71 us (3%)
    pallas_call x1, Pallas kernels, body(): pl.pallas_call(partial(kernel, n), out_shape=pltpu.VMEM((local, width), d...  19.8 us
    unnamed x1, local copies, waits for them, and re-layouts  0.71 us

profile of v5, /device:TPU:0, one launch (start us, length us, event | category | flops | bytes accessed | tf_op | source)
XLA Modules:
  0.0 20.5 jit_solution(12843830682099430459)
XLA Ops:
  0.0 19.8 %shard_map.55 = bf16[32,4096]{1,0:T(8,128)(2,1)S(1)} custom-call(bf16[32,4096]{1,0:T(8,128)(2,1)} %tok_hbm.1, s32[8,32]{1,0:T(8,128)} %bitcast.2, bf16[8,32]{1,0:T(8,128)(2,1)} %bitcast.3, bf16[1,4096,768]{2,1,0:T(8,128)(2,1)} %win_hbm.1, bf16[1,384,4096]{2,1,0:T(8,128)(2,1)} %wout_hbm.1), custom_call_target="tpu_custom_call" | custom-call | tf_op jit(solution)/shard_map/pallas_call | solution.py:309
  19.8 0.7 %copy.7 = bf16[32,4096]{1,0:T(8,128)(2,1)} copy(bf16[32,4096]{1,0:T(8,128)(2,1)S(1)} %shard_map.55) | data formatting | bytes 524288

commit v6 on v4

--- a/solution.py
+++ b/solution.py
@@ -11,7 +11,7 @@
 PACK = 2 * SRC_CAP
 IN_CHUNKS = 2
 OUT_CHUNKS = 2
-RELAY_IN = 0
+RELAY_IN = 1
 RELAY_OUT = 0
 MESH = pl.DeviceIdType.MESH
 
@@ -184,8 +184,10 @@
     combine = jnp.transpose(slot_matrix(weight, routed, position, n * PACK, 2 * PACK))
     combine = jnp.concatenate(split_halves(combine, 1), axis=0).astype(jnp.bfloat16)
 
-    def in_step(c, total):
-        win_copy(c).wait()
+    outer = (me % 2 == 0) == (2 * pair < flight)
+
+    def in_step(step, total):
+        c = jnp.where(outer, IN_CHUNKS - 1 - step, step)
         for src in others():
             relay_copy(src, c).wait_recv()
 
@@ -194,6 +196,7 @@
                 relay_copy(src, c).start()
 
         relay_copy(partner, c).wait_recv()
+        win_copy(c).wait()
         packed = recv_rows[:, c].astype(jnp.float32)
         for half in range(2):
             rows = packed[:, half * SRC_CAP : (half + 1) * SRC_CAP].reshape(n * SRC_CAP, in_half)

time: 20.6 us -> 19.9 us (0.966)
  Pallas kernels: 19.7 us -> 19 us
    pallas_call x1, Pallas kernels: 19.7 us -> 19 us  [body(): pl.pallas_call(partial(kernel, n), out_shape=pltpu.VMEM((local, width), d...]
where the time goes in v6:
time: 19.9 us; the launch traced here: 19.7 us
  Pallas kernels  19 us (95%)
  local copies, waits for them, and re-layouts  0.71 us (4%)
    pallas_call x1, Pallas kernels, body(): pl.pallas_call(partial(kernel, n), out_shape=pltpu.VMEM((local, width), d...  19 us
    unnamed x1, local copies, waits for them, and re-layouts  0.71 us

profile of v6, /device:TPU:0, one launch (start us, length us, event | category | flops | bytes accessed | tf_op | source)
XLA Modules:
  0.0 19.7 jit_solution(18144098865116791760)
XLA Ops:
  0.0 19.0 %shard_map.55 = bf16[32,4096]{1,0:T(8,128)(2,1)S(1)} custom-call(bf16[32,4096]{1,0:T(8,128)(2,1)} %tok_hbm.1, s32[8,32]{1,0:T(8,128)} %bitcast.2, bf16[8,32]{1,0:T(8,128)(2,1)} %bitcast.3, bf16[1,4096,768]{2,1,0:T(8,128)(2,1)} %win_hbm.1, bf16[1,384,4096]{2,1,0:T(8,128)(2,1)} %wout_hbm.1), custom_call_target="tpu_custom_call" | custom-call | tf_op jit(solution)/shard_map/pallas_call | solution.py:307
  19.0 0.7 %copy.7 = bf16[32,4096]{1,0:T(8,128)(2,1)} copy(bf16[32,4096]{1,0:T(8,128)(2,1)S(1)} %shard_map.55) | data formatting | bytes 524288

commit v7 on v6

--- a/solution.py
+++ b/solution.py
@@ -12,7 +12,7 @@
 IN_CHUNKS = 2
 OUT_CHUNKS = 2
 RELAY_IN = 1
-RELAY_OUT = 0
+RELAY_OUT = 1
 MESH = pl.DeviceIdType.MESH
 
 

time: 19.9 us -> 20.9 us (1.050)
  Pallas kernels: 19 us -> 20 us
    pallas_call x1, Pallas kernels: 19 us -> 20 us  [body(): pl.pallas_call(partial(kernel, n), out_shape=pltpu.VMEM((local, width), d...]
where the time goes in v7:
time: 20.9 us; the launch traced here: 20.7 us
  Pallas kernels  20 us (96%)
  local copies, waits for them, and re-layouts  0.71 us (3%)
    pallas_call x1, Pallas kernels, body(): pl.pallas_call(partial(kernel, n), out_shape=pltpu.VMEM((local, width), d...  20 us
    unnamed x1, local copies, waits for them, and re-layouts  0.71 us

profile of v7, /device:TPU:0, one launch (start us, length us, event | category | flops | bytes accessed | tf_op | source)
XLA Modules:
  0.0 20.7 jit_solution(12895724126863235318)
XLA Ops:
  0.0 20.0 %shard_map.55 = bf16[32,4096]{1,0:T(8,128)(2,1)S(1)} custom-call(bf16[32,4096]{1,0:T(8,128)(2,1)} %tok_hbm.1, s32[8,32]{1,0:T(8,128)} %bitcast.2, bf16[8,32]{1,0:T(8,128)(2,1)} %bitcast.3, bf16[1,4096,768]{2,1,0:T(8,128)(2,1)} %win_hbm.1, bf16[1,384,4096]{2,1,0:T(8,128)(2,1)} %wout_hbm.1), custom_call_target="tpu_custom_call" | custom-call | tf_op jit(solution)/shard_map/pallas_call | solution.py:307
  20.0 0.7 %copy.7 = bf16[32,4096]{1,0:T(8,128)(2,1)} copy(bf16[32,4096]{1,0:T(8,128)(2,1)S(1)} %shard_map.55) | data formatting | bytes 524288

commit v8 on v6

--- a/solution.py
+++ b/solution.py
@@ -10,7 +10,7 @@
 SRC_CAP = 8
 PACK = 2 * SRC_CAP
 IN_CHUNKS = 2
-OUT_CHUNKS = 2
+OUT_CHUNKS = 4
 RELAY_IN = 1
 RELAY_OUT = 0
 MESH = pl.DeviceIdType.MESH

time: 19.9 us -> 20.2 us (1.015)
  Pallas kernels: 19 us -> 19.3 us
    pallas_call x1, Pallas kernels: 19 us -> 19.3 us  [body(): pl.pallas_call(partial(kernel, n), out_shape=pltpu.VMEM((local, width), d...]
where the time goes in v8:
time: 20.2 us; the launch traced here: 20 us
  Pallas kernels  19.3 us (96%)
  local copies, waits for them, and re-layouts  0.71 us (4%)
    pallas_call x1, Pallas kernels, body(): pl.pallas_call(partial(kernel, n), out_shape=pltpu.VMEM((local, width), d...  19.3 us
    unnamed x1, local copies, waits for them, and re-layouts  0.71 us

profile of v8, /device:TPU:0, one launch (start us, length us, event | category | flops | bytes accessed | tf_op | source)
XLA Modules:
  0.0 20.0 jit_solution(14338623334643434013)
XLA Ops:
  0.0 19.3 %shard_map.55 = bf16[32,4096]{1,0:T(8,128)(2,1)S(1)} custom-call(bf16[32,4096]{1,0:T(8,128)(2,1)} %tok_hbm.1, s32[8,32]{1,0:T(8,128)} %bitcast.2, bf16[8,32]{1,0:T(8,128)(2,1)} %bitcast.3, bf16[1,4096,768]{2,1,0:T(8,128)(2,1)} %win_hbm.1, bf16[1,384,4096]{2,1,0:T(8,128)(2,1)} %wout_hbm.1), custom_call_target="tpu_custom_call" | custom-call | tf_op jit(solution)/shard_map/pallas_call | solution.py:307
  19.3 0.7 %copy.7 = bf16[32,4096]{1,0:T(8,128)(2,1)} copy(bf16[32,4096]{1,0:T(8,128)(2,1)S(1)} %shard_map.55) | data formatting | bytes 524288

commit v9 on v6

--- a/solution.py
+++ b/solution.py
@@ -101,13 +101,16 @@
         copy.start()
 
     def win_copy(c):
-        rows = pl.ds(c * in_width, in_width)
+        rows = pl.ds(pl.multiple_of(c * in_width, in_width), in_width)
         return pltpu.make_async_copy(win_hbm.at[0, rows], win.at[rows], win_sem.at[c])
 
     wout_copy = pltpu.make_async_copy(wout_hbm.at[0], wout, wout_sem)
-    for c in range(IN_CHUNKS):
-        win_copy(c).start()
-    wout_copy.start()
+    outer = (me % 2 == 0) == (2 * pair < flight)
+
+    def chunk_at(step):
+        return jnp.where(outer, IN_CHUNKS - 1 - step, step)
+
+    win_copy(chunk_at(0)).start()
 
     small[0].wait()
     small[1].wait()
@@ -181,13 +184,15 @@
             row_copy(dst, c).start()
         recv_rows[me, c] = send_rows[me // 2, c]
 
+    for step in range(1, IN_CHUNKS):
+        win_copy(chunk_at(step)).start()
+    wout_copy.start()
+
     combine = jnp.transpose(slot_matrix(weight, routed, position, n * PACK, 2 * PACK))
     combine = jnp.concatenate(split_halves(combine, 1), axis=0).astype(jnp.bfloat16)
 
-    outer = (me % 2 == 0) == (2 * pair < flight)
-
     def in_step(step, total):
-        c = jnp.where(outer, IN_CHUNKS - 1 - step, step)
+        c = chunk_at(step)
         for src in others():
             relay_copy(src, c).wait_recv()
 

time: 19.9 us -> 19.9 us (level)
  no operation moved by 1% of the time
where the time goes in v9:
time: 19.9 us; the launch traced here: 19.7 us
  Pallas kernels  19 us (95%)
  local copies, waits for them, and re-layouts  0.71 us (4%)
    pallas_call x1, Pallas kernels, body(): pl.pallas_call(partial(kernel, n), out_shape=pltpu.VMEM((local, width), d...  19 us
    unnamed x1, local copies, waits for them, and re-layouts  0.71 us

profile of v9, /device:TPU:0, one launch (start us, length us, event | category | flops | bytes accessed | tf_op | source)
XLA Modules:
  0.0 19.7 jit_solution(16652195691681763055)
XLA Ops:
  0.0 19.0 %shard_map.55 = bf16[32,4096]{1,0:T(8,128)(2,1)S(1)} custom-call(bf16[32,4096]{1,0:T(8,128)(2,1)} %tok_hbm.1, s32[8,32]{1,0:T(8,128)} %bitcast.2, bf16[8,32]{1,0:T(8,128)(2,1)} %bitcast.3, bf16[1,4096,768]{2,1,0:T(8,128)(2,1)} %win_hbm.1, bf16[1,384,4096]{2,1,0:T(8,128)(2,1)} %wout_hbm.1), custom_call_target="tpu_custom_call" | custom-call | tf_op jit(solution)/shard_map/pallas_call | solution.py:312
  19.0 0.7 %copy.7 = bf16[32,4096]{1,0:T(8,128)(2,1)} copy(bf16[32,4096]{1,0:T(8,128)(2,1)S(1)} %shard_map.55) | data formatting | bytes 524288

commit v10 on v7

--- a/solution.py
+++ b/solution.py
@@ -71,6 +71,7 @@
     out_width = width // OUT_CHUNKS
     out_half = out_width // 2
 
+    lean = lax.axis_index("dp") % 2 == 1
     pair = me // 2
     partner = me + 1 - 2 * (me % 2)
 
@@ -155,13 +156,17 @@
             device_id_type=MESH,
         )
 
-    def row_targets(c):
+    def for_row_targets(c, act):
         for k in range(1, flight):
             near = near_of(me, other_pair(k))
-            yield near
+            act(row_copy(near, c))
             if c >= RELAY_IN:
-                yield 4 * other_pair(k) + 1 - near
-        yield partner
+
+                @pl.when(jnp.logical_not(lean))
+                def _():
+                    act(row_copy(4 * other_pair(k) + 1 - near, c))
+
+        act(row_copy(partner, c))
 
     small[2].wait()
     for c in range(IN_CHUNKS):
@@ -177,21 +182,20 @@
         send_rows[:, c] = rows.reshape(flight, PACK, in_half)
         if c == 0:
             pl.semaphore_wait(barrier, n - 1)
-        for dst in row_targets(c):
-            row_copy(dst, c).start()
+        for_row_targets(c, lambda copy: copy.start())
         recv_rows[me, c] = send_rows[me // 2, c]
 
     combine = jnp.transpose(slot_matrix(weight, routed, position, n * PACK, 2 * PACK))
     combine = jnp.concatenate(split_halves(combine, 1), axis=0).astype(jnp.bfloat16)
 
-    outer = (me % 2 == 0) == (2 * pair < flight)
+    outer = ((me % 2 == 0) == (2 * pair < flight)) & jnp.logical_not(lean)
 
     def in_step(step, total):
         c = jnp.where(outer, IN_CHUNKS - 1 - step, step)
         for src in others():
             relay_copy(src, c).wait_recv()
 
-            @pl.when((near_of(src, pair) == me) & (c < RELAY_IN))
+            @pl.when((near_of(src, pair) == me) & (lean | (c < RELAY_IN)))
             def _():
                 relay_copy(src, c).start()
 
@@ -245,9 +249,13 @@
         for dst in others():
             if c < RELAY_OUT:
 
-                @pl.when(near_of(dst, pair) != me)
+                @pl.when(lean & (near_of(dst, pair) != me))
                 def _():
                     partial_copy(dst, c).start()
+
+                @pl.when(jnp.logical_not(lean))
+                def _():
+                    out_copy(dst, c, me).start()
             else:
                 out_copy(dst, c, me).start()
         out_copy(partner, c, me).start()
@@ -256,7 +264,7 @@
     for c in range(RELAY_OUT):
         for dst in others():
 
-            @pl.when(near_of(dst, pair) == me)
+            @pl.when(lean & (near_of(dst, pair) == me))
             def _():
                 partial_copy(dst, c).wait_recv()
                 both = send_out[dst, c].astype(jnp.float32) + partial_out[dst, c].astype(
@@ -266,29 +274,34 @@
                 out_copy(dst, c, 2 * pair).start()
 
         for k in range(1, flight):
-            recv_out[2 * other_pair(k) + 1, c] = jnp.zeros((PACK, out_half), recv_out.dtype)
-
-    for c in list(range(RELAY_OUT, OUT_CHUNKS)) + list(range(RELAY_OUT)):
-        lo = c * out_width
+
+            @pl.when(lean)
+            def _():
+                recv_out[2 * other_pair(k) + 1, c] = jnp.zeros((PACK, out_half), recv_out.dtype)
+
+    for step in range(OUT_CHUNKS):
+        c = jnp.where(lean, OUT_CHUNKS - 1 - step, step)
         out_copy(partner, c, partner).wait_recv()
         for k in range(1, flight):
             out_copy(partner, c, 2 * other_pair(k)).wait_recv()
-            if c >= RELAY_OUT:
+
+            @pl.when(jnp.logical_not(lean) | (c >= RELAY_OUT))
+            def _():
                 out_copy(partner, c, 2 * other_pair(k) + 1).wait_recv()
+
         packed = recv_out[:, c].reshape(n * PACK, out_half)
         mixed = jnp.dot(combine, packed, preferred_element_type=jnp.float32).astype(jnp.bfloat16)
-        out_ref[:, lo : lo + out_half] = mixed[:tokens]
-        out_ref[:, lo + out_half : lo + out_width] = mixed[tokens:]
+        for half in range(2):
+            lo = pl.multiple_of(c * out_width + half * out_half, out_half)
+            out_ref[:, pl.ds(lo, out_half)] = mixed[half * tokens : (half + 1) * tokens]
 
     for c in range(IN_CHUNKS):
-        for dst in row_targets(c):
-            row_copy(dst, c).wait_send()
-        if c < RELAY_IN:
-            for src in others():
-
-                @pl.when(near_of(src, pair) == me)
-                def _():
-                    relay_copy(src, c).wait_send()
+        for_row_targets(c, lambda copy: copy.wait_send())
+        for src in others():
+
+            @pl.when((near_of(src, pair) == me) & (lean | (c < RELAY_IN)))
+            def _():
+                relay_copy(src, c).wait_send()
 
     for c in range(OUT_CHUNKS):
         for dst in others():

time: 20.9 us -> 19.9 us (0.952)
  Pallas kernels: 20 us -> 19 us
    pallas_call x1, Pallas kernels: 20 us -> 19 us  [body(): pl.pallas_call(partial(kernel, n), out_shape=pltpu.VMEM((local, width), d...]
where the time goes in v10:
time: 19.9 us; the launch traced here: 19.7 us
  Pallas kernels  19 us (95%)
  local copies, waits for them, and re-layouts  0.71 us (4%)
    pallas_call x1, Pallas kernels, body(): pl.pallas_call(partial(kernel, n), out_shape=pltpu.VMEM((local, width), d...  19 us
    unnamed x1, local copies, waits for them, and re-layouts  0.71 us

profile of v10, /device:TPU:0, one launch (start us, length us, event | category | flops | bytes accessed | tf_op | source)
XLA Modules:
  0.0 19.7 jit_solution(16537573147619382343)
XLA Ops:
  0.0 19.0 %shard_map.55 = bf16[32,4096]{1,0:T(8,128)(2,1)S(1)} custom-call(bf16[32,4096]{1,0:T(8,128)(2,1)} %tok_hbm.1, s32[8,32]{1,0:T(8,128)} %bitcast.2, bf16[8,32]{1,0:T(8,128)(2,1)} %bitcast.3, bf16[1,4096,768]{2,1,0:T(8,128)(2,1)} %win_hbm.1, bf16[1,384,4096]{2,1,0:T(8,128)(2,1)} %wout_hbm.1), custom_call_target="tpu_custom_call" | custom-call | tf_op jit(solution)/shard_map/pallas_call | solution.py:320
  19.0 0.7 %copy.7 = bf16[32,4096]{1,0:T(8,128)(2,1)} copy(bf16[32,4096]{1,0:T(8,128)(2,1)S(1)} %shard_map.55) | data formatting | bytes 524288

commit v11 on v2

--- a/solution.py
+++ b/solution.py
@@ -9,8 +9,9 @@
 
 SRC_CAP = 8
 PACK = 2 * SRC_CAP
-IN_CHUNKS = 4
-OUT_CHUNKS = 4
+IN_CHUNKS = 2
+OUT_CHUNKS = 2
+RELAY_IN = 1
 MESH = pl.DeviceIdType.MESH
 
 
@@ -56,6 +57,7 @@
     row_recv_sem,
     out_send_sem,
     out_recv_sem,
+    relay_sem,
 ):
     me = lax.axis_index("expert")
     flight = n // 2
@@ -66,12 +68,18 @@
     out_width = width // OUT_CHUNKS
     out_half = out_width // 2
 
-    def peer(d):
-        return lax.rem(me + d, n)
-
-    barrier = pltpu.get_barrier_semaphore()
-    for d in range(1, n):
-        pl.semaphore_signal(barrier, inc=1, device_id={"expert": peer(d)}, device_id_type=MESH)
+    pair = me // 2
+    partner = me + 1 - 2 * (me % 2)
+
+    def wrapped(index, count):
+        return jnp.where(index >= count, index - count, index)
+
+    peers = [wrapped(me + d, n) for d in range(1, n)]
+    other_pairs = [wrapped(pair + k, flight) for k in range(1, flight)]
+    others = [2 * other + member for other in other_pairs for member in range(2)]
+    nears = [2 * other + jnp.where(me < 2 * other, 0, 1) for other in other_pairs]
+    fars = [4 * other + 1 - near for other, near in zip(other_pairs, nears)]
+    near_to = [(other < pair) == (me == 2 * pair) for other in other_pairs for _ in range(2)]
 
     small = [
         pltpu.make_async_copy(ids_hbm, ids, small_sem.at[0]),
@@ -80,6 +88,10 @@
     ]
     for copy in small:
         copy.start()
+
+    barrier = pltpu.get_barrier_semaphore()
+    for peer in peers:
+        pl.semaphore_signal(barrier, inc=1, device_id={"expert": peer}, device_id_type=MESH)
 
     def win_copy(c):
         rows = pl.ds(c * in_width, in_width)
@@ -116,8 +128,7 @@
     pick = slot_matrix(routed, routed, position, flight * PACK, PACK)
     pick = [part.astype(jnp.bfloat16) for part in split_halves(pick, 0)]
 
-    def row_copy(d, c):
-        dst = peer(d)
+    def row_copy(dst, c):
         return pltpu.make_async_remote_copy(
             src_ref=send_rows.at[dst // 2, c],
             dst_ref=recv_rows.at[me, c],
@@ -127,16 +138,18 @@
             device_id_type=MESH,
         )
 
-    def row_arrival(d, c):
-        src = peer(d)
+    def relay_copy(src, c):
         return pltpu.make_async_remote_copy(
-            src_ref=send_rows.at[0, c],
+            src_ref=recv_rows.at[src, c],
             dst_ref=recv_rows.at[src, c],
-            send_sem=row_send_sem.at[src, c],
+            send_sem=relay_sem.at[src, c],
             recv_sem=row_recv_sem.at[src, c],
-            device_id={"expert": src},
+            device_id={"expert": partner},
             device_id_type=MESH,
         )
+
+    def row_targets(c):
+        return nears + (fars if c >= RELAY_IN else []) + [partner]
 
     small[2].wait()
     for c in range(IN_CHUNKS):
@@ -152,53 +165,47 @@
         send_rows[:, c] = rows.reshape(flight, PACK, in_half)
         if c == 0:
             pl.semaphore_wait(barrier, n - 1)
-        for d in range(1, n):
-            row_copy(d, c).start()
+        for dst in row_targets(c):
+            row_copy(dst, c).start()
         recv_rows[me, c] = send_rows[me // 2, c]
 
     combine = jnp.transpose(slot_matrix(weight, routed, position, n * PACK, 2 * PACK))
     combine = jnp.concatenate(split_halves(combine, 1), axis=0).astype(jnp.bfloat16)
 
-    def in_step(c, total):
+    outer = (me % 2 == 0) == (2 * pair < flight)
+
+    merged = jnp.zeros((n * SRC_CAP, 2 * hid), jnp.float32)
+    for step in range(IN_CHUNKS):
+        c = jnp.where(outer, IN_CHUNKS - 1 - step, step)
+        for src, near in zip(others, near_to):
+            relay_copy(src, c).wait_recv()
+
+            @pl.when(near & (c < RELAY_IN))
+            def _():
+                relay_copy(src, c).start()
+
+        relay_copy(partner, c).wait_recv()
         win_copy(c).wait()
-        for d in range(1, n):
-            row_arrival(d, c).wait_recv()
         packed = recv_rows[:, c].astype(jnp.float32)
         for half in range(2):
             rows = packed[:, half * SRC_CAP : (half + 1) * SRC_CAP].reshape(n * SRC_CAP, in_half)
             start = pl.multiple_of(c * in_width + half * in_half, in_half)
-            total = total + jnp.dot(
+            merged = merged + jnp.dot(
                 rows.astype(jnp.bfloat16),
                 win[pl.ds(start, in_half)],
                 preferred_element_type=jnp.float32,
             )
-        return total
-
-    merged = lax.fori_loop(
-        0, IN_CHUNKS, in_step, jnp.zeros((n * SRC_CAP, 2 * hid), jnp.float32)
-    )
+
     left = merged[:, :hid]
     hidden = (left / (1.0 + jnp.exp(-left)) * merged[:, hid:]).astype(jnp.bfloat16)
 
-    def out_copy(d, c):
-        dst = peer(d)
+    def out_copy(dst, c, slot):
         return pltpu.make_async_remote_copy(
             src_ref=send_out.at[dst, c],
-            dst_ref=recv_out.at[me, c],
+            dst_ref=recv_out.at[slot, c],
             send_sem=out_send_sem.at[dst, c],
-            recv_sem=out_recv_sem.at[me, c],
+            recv_sem=out_recv_sem.at[slot, c],
             device_id={"expert": dst},
-            device_id_type=MESH,
-        )
-
-    def out_arrival(d, c):
-        src = peer(d)
-        return pltpu.make_async_remote_copy(
-            src_ref=send_out.at[src, c],
-            dst_ref=recv_out.at[src, c],
-            send_sem=out_send_sem.at[src, c],
-            recv_sem=out_recv_sem.at[src, c],
-            device_id={"expert": src},
             device_id_type=MESH,
         )
 
@@ -210,25 +217,31 @@
         ).reshape(n, SRC_CAP, out_width)
         packed = jnp.concatenate([output[:, :, :out_half], output[:, :, out_half:]], axis=1)
         send_out[:, c] = packed.astype(jnp.bfloat16)
-        for d in range(1, n):
-            out_copy(d, c).start()
+        for dst in others:
+            out_copy(dst, c, me).start()
+        out_copy(partner, c, me).start()
         recv_out[me, c] = send_out[me, c]
+
+    for c in range(IN_CHUNKS):
+        for dst in row_targets(c):
+            row_copy(dst, c).wait_send()
+        if c < RELAY_IN:
+            for src, near in zip(others, near_to):
+
+                @pl.when(near)
+                def _():
+                    relay_copy(src, c).wait_send()
 
     for c in range(OUT_CHUNKS):
         lo = c * out_width
-        for d in range(1, n):
-            out_arrival(d, c).wait_recv()
+        for peer in others + [partner]:
+            out_copy(peer, c, me).wait_send()
+        for peer in others + [partner]:
+            out_copy(partner, c, peer).wait_recv()
         packed = recv_out[:, c].reshape(n * PACK, out_half)
         mixed = jnp.dot(combine, packed, preferred_element_type=jnp.float32).astype(jnp.bfloat16)
         out_ref[:, lo : lo + out_half] = mixed[:tokens]
         out_ref[:, lo + out_half : lo + out_width] = mixed[tokens:]
-
-    for c in range(IN_CHUNKS):
-        for d in range(1, n):
-            row_copy(d, c).wait_send()
-    for c in range(OUT_CHUNKS):
-        for d in range(1, n):
-            out_copy(d, c).wait_send()
 
 
 def body(tokens, expert_ids, gates, weights_in, weights_out):
@@ -261,6 +274,7 @@
             pltpu.SemaphoreType.DMA((n, IN_CHUNKS)),
             pltpu.SemaphoreType.DMA((n, OUT_CHUNKS)),
             pltpu.SemaphoreType.DMA((n, OUT_CHUNKS)),
+            pltpu.SemaphoreType.DMA((n, IN_CHUNKS)),
         ],
         compiler_params=pltpu.CompilerParams(
             collective_id=0, has_side_effects=True, vmem_limit_bytes=56 * 2**20

time: 21 us -> 19.8 us (0.943)
  Pallas kernels: 20.1 us -> 18.9 us
    pallas_call x1, Pallas kernels: 20.1 us -> 18.9 us  [body(): pl.pallas_call(partial(kernel, n), out_shape=pltpu.VMEM((local, width), d...]
where the time goes in v11:
time: 19.8 us; the launch traced here: 19.6 us
  Pallas kernels  18.9 us (95%)
  local copies, waits for them, and re-layouts  0.71 us (4%)
    pallas_call x1, Pallas kernels, body(): pl.pallas_call(partial(kernel, n), out_shape=pltpu.VMEM((local, width), d...  18.9 us
    unnamed x1, local copies, waits for them, and re-layouts  0.71 us

profile of v11, /device:TPU:0, one launch (start us, length us, event | category | flops | bytes accessed | tf_op | source)
XLA Modules:
  0.0 19.6 jit_solution(1461662851890678842)
XLA Ops:
  0.0 18.9 %shard_map.55 = bf16[32,4096]{1,0:T(8,128)(2,1)S(1)} custom-call(bf16[32,4096]{1,0:T(8,128)(2,1)} %tok_hbm.1, s32[8,32]{1,0:T(8,128)} %bitcast.2, bf16[8,32]{1,0:T(8,128)(2,1)} %bitcast.3, bf16[1,4096,768]{2,1,0:T(8,128)(2,1)} %win_hbm.1, bf16[1,384,4096]{2,1,0:T(8,128)(2,1)} %wout_hbm.1), custom_call_target="tpu_custom_call" | custom-call | tf_op jit(solution)/shard_map/pallas_call | solution.py:255
  18.9 0.7 %copy.7 = bf16[32,4096]{1,0:T(8,128)(2,1)} copy(bf16[32,4096]{1,0:T(8,128)(2,1)S(1)} %shard_map.55) | data formatting | bytes 524288

commit v12 on v11

v12 whole, which is shorter than its diff:
```python
from functools import partial

import jax
import jax.numpy as jnp
from jax import lax
from jax.experimental import pallas as pl
from jax.experimental.pallas import tpu as pltpu
from jax.sharding import PartitionSpec as P

SRC_CAP = 8
PACK = 2 * SRC_CAP
GROUPS = 2
SLOTS = SRC_CAP // GROUPS
PARTS = PACK // SLOTS
RELAY = 1
MESH = pl.DeviceIdType.MESH


def slot_matrix(value, routed, position, rows, rows_per_expert, group):
    tokens = value[0].shape[1]
    row = lax.broadcasted_iota(jnp.int32, (rows, tokens), 0)
    slot = (row % SLOTS + group * SLOTS).astype(jnp.float32)
    expert = row // rows_per_expert
    table = jnp.zeros((rows, tokens), jnp.float32)
    for e in range(len(value)):
        hit = (expert == e) & (position[e] == slot) & (routed[e] > 0.0)
        table = jnp.where(hit, value[e], table)
    return table


def split_parts(table, axis):
    part = (lax.broadcasted_iota(jnp.int32, table.shape, axis) // SLOTS) % PARTS
    return [jnp.where(part == p, table, jnp.zeros_like(table)) for p in range(PARTS)]


def kernel(
    n,
    tok_hbm,
    ids_hbm,
    gate_hbm,
    win_hbm,
    wout_hbm,
    out_ref,
    tok,
    ids,
    gate,
    win,
    wout,
    send_rows,
    recv_rows,
    send_out,
    recv_out,
    small_sem,
    win_sem,
    wout_sem,
    row_send_sem,
    row_recv_sem,
    out_send_sem,
    out_recv_sem,
    relay_sem,
):
    me = lax.axis_index("expert")
    flight = n // 2
    width = tok.shape[1]
    hid = wout.shape[0]
    part_width = width // PARTS
    half_width = width // 2
    pair = me // 2
    partner = me + 1 - 2 * (me % 2)

    def wrapped(index, count):
        return jnp.where(index >= count, index - count, index)

    peers = [wrapped(me + d, n) for d in range(1, n)]
    other_pairs = [wrapped(pair + k, flight) for k in range(1, flight)]
    others = [2 * other + member for other in other_pairs for member in range(2)]
    nears = [2 * other + jnp.where(me < 2 * other, 0, 1) for other in other_pairs]
    fars = [4 * other + 1 - near for other, near in zip(other_pairs, nears)]
    near_to = [(other < pair) == (me == 2 * pair) for other in other_pairs for _ in range(2)]

    small = [
        pltpu.make_async_copy(ids_hbm, ids, small_sem.at[0]),
        pltpu.make_async_copy(gate_hbm, gate, small_sem.at[1]),
        pltpu.make_async_copy(tok_hbm, tok, small_sem.at[2]),
    ]
    for copy in small:
        copy.start()

    barrier = pltpu.get_barrier_semaphore()
    for peer in peers:
        pl.semaphore_signal(barrier, inc=1, device_id={"expert": peer}, device_id_type=MESH)

    def win_copy(c):
        rows = pl.ds(c * half_width, half_width)
        return pltpu.make_async_copy(win_hbm.at[0, rows], win.at[rows], win_sem.at[c])

    wout_copy = pltpu.make_async_copy(wout_hbm.at[0], wout, wout_sem)
    for c in range(2):
        win_copy(c).start()
    wout_copy.start()

    small[0].wait()
    small[1].wait()
    chosen = ids[...]
    gates = gate[...].astype(jnp.float32)
    tokens = chosen.shape[1]
    weight, routed = [], []
    for e in range(flight):
        match = chosen == e
        weight.append(jnp.sum(jnp.where(match, gates, 0.0), axis=0, keepdims=True))
        routed.append(jnp.sum(jnp.where(match, 1.0, 0.0), axis=0, keepdims=True))
    row = lax.broadcasted_iota(jnp.int32, (PACK, tokens), 0)
    marks = jnp.zeros((PACK, tokens), jnp.float32)
    for e in range(flight):
        marks = jnp.where(row == e, routed[e], marks)
    before = lax.broadcasted_iota(jnp.int32, (tokens, tokens), 0) < lax.broadcasted_iota(
        jnp.int32, (tokens, tokens), 1
    )
    ahead = jnp.dot(
        marks.astype(jnp.bfloat16),
        before.astype(jnp.float32).astype(jnp.bfloat16),
        preferred_element_type=jnp.float32,
    )
    position = [ahead[e : e + 1] for e in range(flight)]
    pick = [
        [
            part.astype(jnp.bfloat16)
            for part in split_parts(
                slot_matrix(routed, routed, position, flight * PACK, PACK, g), 0
            )
        ]
        for g in range(GROUPS)
    ]

    def row_copy(dst, c):
        return pltpu.make_async_remote_copy(
            src_ref=send_rows.at[dst // 2, c],
            dst_ref=recv_rows.at[me, c],
            send_sem=row_send_sem.at[dst, c],
            recv_sem=row_recv_sem.at[me, c],
            device_id={"expert": dst},
            device_id_type=MESH,
        )

    def relay_copy(src, c):
        return pltpu.make_async_remote_copy(
            src_ref=recv_rows.at[src, c],
            dst_ref=recv_rows.at[src, c],
            send_sem=relay_sem.at[src, c],
            recv_sem=row_recv_sem.at[src, c],
            device_id={"expert": partner},
            device_id_type=MESH,
        )

    def row_targets(c):
        return nears + (fars if c >= RELAY else []) + [partner]

    small[2].wait()
    for c in range(GROUPS):
        rows = sum(
            jnp.dot(
                pick[c][p],
                tok[:, p * part_width : (p + 1) * part_width],
                preferred_element_type=jnp.float32,
            )
            for p in range(PARTS)
        ).astype(jnp.bfloat16)
        send_rows[:, c] = rows.reshape(flight, PACK, part_width)
        if c == 0:
            pl.semaphore_wait(barrier, n - 1)
        for dst in row_targets(c):
            row_copy(dst, c).start()
        recv_rows[me, c] = send_rows[me // 2, c]

    combine = []
    for g in range(GROUPS):
        table = slot_matrix(weight, routed, position, n * PACK, 2 * PACK, g)
        combine.append(jnp.concatenate(split_parts(jnp.transpose(table), 1), axis=0))
    combine = [table.astype(jnp.bfloat16) for table in combine]

    outer = (me % 2 == 0) == (2 * pair < flight)

    def out_copy(dst, c, slot):
        return pltpu.make_async_remote_copy(
            src_ref=send_out.at[dst, c],
            dst_ref=recv_out.at[slot, c],
            send_sem=out_send_sem.at[dst, c],
            recv_sem=out_recv_sem.at[slot, c],
            device_id={"expert": dst},
            device_id_type=MESH,
        )

    for step in range(GROUPS):
        c = jnp.where(outer, GROUPS - 1 - step, step)
        for src, near in zip(others, near_to):
            relay_copy(src, c).wait_recv()

            @pl.when(near & (c < RELAY))
            def _():
                relay_copy(src, c).start()

        relay_copy(partner, c).wait_recv()
        if step == 0:
            win_copy(0).wait()
            win_copy(1).wait()
        packed = recv_rows[:, c].reshape(n * PACK, part_width).astype(jnp.float32)
        merged = jnp.zeros((n * PACK, 2 * hid), jnp.float32)
        for p, rows in enumerate(split_parts(packed, 0)):
            merged = merged + jnp.dot(
                rows.astype(jnp.bfloat16),
                win[p * part_width : (p + 1) * part_width],
                preferred_element_type=jnp.float32,
            )
        merged = merged.reshape(n, PACK, 2 * hid)
        merged = (merged[:, :SRC_CAP] + merged[:, SRC_CAP:]).reshape(n * SRC_CAP, 2 * hid)
        swapped = merged.reshape(n, SRC_CAP, 2 * hid)
        swapped = pltpu.roll(swapped, SLOTS, 1).reshape(n * SRC_CAP, 2 * hid)
        merged = merged + swapped
        left = merged[:, :hid]
        hidden = (left / (1.0 + jnp.exp(-left)) * merged[:, hid:]).astype(jnp.bfloat16)

        if step == 0:
            wout_copy.wait()
        first = lax.broadcasted_iota(jnp.int32, (n, SRC_CAP, part_width), 1) < SLOTS
        for half in range(2):
            output = [
                jnp.dot(
                    hidden,
                    wout[:, p * part_width : (p + 1) * part_width],
                    preferred_element_type=jnp.float32,
                ).reshape(n, SRC_CAP, part_width)
                for p in (2 * half, 2 * half + 1)
            ]
            if half == 0:
                lower = jnp.where(first, output[0], output[1])
            else:
                upper = jnp.where(first, output[0], output[1])
        send_out[:, c] = jnp.concatenate([lower, upper], axis=1).astype(jnp.bfloat16)
        for peer in others + [partner]:
            out_copy(peer, c, me).start()
        recv_out[me, c] = send_out[me, c]

    for c in range(GROUPS):
        for dst in row_targets(c):
            row_copy(dst, c).wait_send()
        if c < RELAY:
            for src, near in zip(others, near_to):

                @pl.when(near)
                def _():
                    relay_copy(src, c).wait_send()

    for c in range(GROUPS):
        for peer in others + [partner]:
            out_copy(peer, c, me).wait_send()
        for peer in others + [partner]:
            out_copy(partner, c, peer).wait_recv()
    mixed = sum(
        jnp.dot(
            combine[g],
            recv_out[:, g].reshape(n * PACK, part_width),
            preferred_element_type=jnp.float32,
        )
        for g in range(GROUPS)
    ).astype(jnp.bfloat16)
    for p in range(PARTS):
        out_ref[:, p * part_width : (p + 1) * part_width] = mixed[p * tokens : (p + 1) * tokens]


def body(tokens, expert_ids, gates, weights_in, weights_out):
    n = lax.axis_size("expert")
    flight = n // 2
    local, width = tokens.shape
    hid = weights_out.shape[1]
    part_width = width // PARTS
    dtype = tokens.dtype
    return pl.pallas_call(
        partial(kernel, n),
        out_shape=pltpu.VMEM((local, width), dtype),
        in_specs=[pl.BlockSpec(memory_space=pltpu.HBM)] * 5,
        out_specs=pl.BlockSpec(memory_space=pltpu.VMEM),
        scratch_shapes=[
            pltpu.VMEM((local, width), dtype),
            pltpu.VMEM(expert_ids.shape[::-1], expert_ids.dtype),
            pltpu.VMEM(gates.shape[::-1], gates.dtype),
            pltpu.VMEM(weights_in.shape[1:], weights_in.dtype),
            pltpu.VMEM(weights_out.shape[1:], weights_out.dtype),
            pltpu.VMEM((flight, GROUPS, PACK, part_width), dtype),
            pltpu.VMEM((n, GROUPS, PACK, part_width), dtype),
            pltpu.VMEM((n, GROUPS, PACK, part_width), dtype),
            pltpu.VMEM((n, GROUPS, PACK, part_width), dtype),
            pltpu.SemaphoreType.DMA((3,)),
            pltpu.SemaphoreType.DMA((2,)),
            pltpu.SemaphoreType.DMA,
            pltpu.SemaphoreType.DMA((n, GROUPS)),
            pltpu.SemaphoreType.DMA((n, GROUPS)),
            pltpu.SemaphoreType.DMA((n, GROUPS)),
            pltpu.SemaphoreType.DMA((n, GROUPS)),
            pltpu.SemaphoreType.DMA((n, GROUPS)),
        ],
        compiler_params=pltpu.CompilerParams(
            collective_id=0, has_side_effects=True, vmem_limit_bytes=56 * 2**20
        ),
    )(tokens, expert_ids.T, gates.T, weights_in, weights_out)


def solution(mesh):
    return jax.shard_map(
        body,
        mesh=mesh,
        in_specs=(
            P(("dp", "expert"), None),
            P(("dp", "expert"), None),
            P(("dp", "expert"), None),
            P("expert", None, None),
            P("expert", None, None),
        ),
        out_specs=P(("dp", "expert"), None),
        check_vma=False,
    )
```

time: 19.8 us -> 20.5 us (1.035)
  Pallas kernels: 18.9 us -> 19.6 us
    pallas_call x1, Pallas kernels: 18.9 us -> 19.6 us  [body(): pl.pallas_call(partial(kernel, n), out_shape=pltpu.VMEM((local, width), d...]
where the time goes in v12:
time: 20.5 us; the launch traced here: 20.4 us
  Pallas kernels  19.6 us (96%)
  local copies, waits for them, and re-layouts  0.71 us (3%)
    pallas_call x1, Pallas kernels, body(): pl.pallas_call(partial(kernel, n), out_shape=pltpu.VMEM((local, width), d...  19.6 us
    unnamed x1, local copies, waits for them, and re-layouts  0.71 us

profile of v12, /device:TPU:0, one launch (start us, length us, event | category | flops | bytes accessed | tf_op | source)
XLA Modules:
  0.0 20.4 jit_solution(12278760730699297976)
XLA Ops:
  0.0 19.6 %shard_map.55 = bf16[32,4096]{1,0:T(8,128)(2,1)S(1)} custom-call(bf16[32,4096]{1,0:T(8,128)(2,1)} %tok_hbm.1, s32[8,32]{1,0:T(8,128)} %bitcast.2, bf16[8,32]{1,0:T(8,128)(2,1)} %bitcast.3, bf16[1,4096,768]{2,1,0:T(8,128)(2,1)} %win_hbm.1, bf16[1,384,4096]{2,1,0:T(8,128)(2,1)} %wout_hbm.1), custom_call_target="tpu_custom_call" | custom-call | tf_op jit(solution)/shard_map/pallas_call | solution.py:277
  19.7 0.7 %copy.7 = bf16[32,4096]{1,0:T(8,128)(2,1)} copy(bf16[32,4096]{1,0:T(8,128)(2,1)S(1)} %shard_map.55) | data formatting | bytes 524288

commit v13 on v11

--- a/solution.py
+++ b/solution.py
@@ -149,7 +149,7 @@
         )
 
     def row_targets(c):
-        return nears + (fars if c >= RELAY_IN else []) + [partner]
+        return (fars if c >= RELAY_IN else []) + nears + [partner]
 
     small[2].wait()
     for c in range(IN_CHUNKS):

time: 19.8 us -> 19.8 us (level)
  no operation moved by 1% of the time
where the time goes in v13:
time: 19.8 us; the launch traced here: 19.6 us
  Pallas kernels  18.9 us (95%)
  local copies, waits for them, and re-layouts  0.71 us (4%)
    pallas_call x1, Pallas kernels, body(): pl.pallas_call(partial(kernel, n), out_shape=pltpu.VMEM((local, width), d...  18.9 us
    unnamed x1, local copies, waits for them, and re-layouts  0.71 us

profile of v13, /device:TPU:0, one launch (start us, length us, event | category | flops | bytes accessed | tf_op | source)
XLA Modules:
  0.0 19.6 jit_solution(6494753473063600845)
XLA Ops:
  0.0 18.9 %shard_map.55 = bf16[32,4096]{1,0:T(8,128)(2,1)S(1)} custom-call(bf16[32,4096]{1,0:T(8,128)(2,1)} %tok_hbm.1, s32[8,32]{1,0:T(8,128)} %bitcast.2, bf16[8,32]{1,0:T(8,128)(2,1)} %bitcast.3, bf16[1,4096,768]{2,1,0:T(8,128)(2,1)} %win_hbm.1, bf16[1,384,4096]{2,1,0:T(8,128)(2,1)} %wout_hbm.1), custom_call_target="tpu_custom_call" | custom-call | tf_op jit(solution)/shard_map/pallas_call | solution.py:255
  18.9 0.7 %copy.7 = bf16[32,4096]{1,0:T(8,128)(2,1)} copy(bf16[32,4096]{1,0:T(8,128)(2,1)S(1)} %shard_map.55) | data formatting | bytes 524288

commit v14 on v13

--- a/solution.py
+++ b/solution.py
@@ -9,9 +9,9 @@
 
 SRC_CAP = 8
 PACK = 2 * SRC_CAP
-IN_CHUNKS = 2
+IN_CHUNKS = 4
 OUT_CHUNKS = 2
-RELAY_IN = 1
+RELAY_IN = 2
 MESH = pl.DeviceIdType.MESH
 
 
@@ -176,7 +176,7 @@
 
     merged = jnp.zeros((n * SRC_CAP, 2 * hid), jnp.float32)
     for step in range(IN_CHUNKS):
-        c = jnp.where(outer, IN_CHUNKS - 1 - step, step)
+        c = jnp.where(outer, (step + RELAY_IN) % IN_CHUNKS, step)
         for src, near in zip(others, near_to):
             relay_copy(src, c).wait_recv()
 

time: 19.8 us -> 19.7 us (level)
  no operation moved by 1% of the time
where the time goes in v14:
time: 19.7 us; the launch traced here: 19.5 us
  Pallas kernels  18.8 us (95%)
  local copies, waits for them, and re-layouts  0.71 us (4%)
    pallas_call x1, Pallas kernels, body(): pl.pallas_call(partial(kernel, n), out_shape=pltpu.VMEM((local, width), d...  18.8 us
    unnamed x1, local copies, waits for them, and re-layouts  0.71 us

profile of v14, /device:TPU:0, one launch (start us, length us, event | category | flops | bytes accessed | tf_op | source)
XLA Modules:
  0.0 19.5 jit_solution(6641397430374989753)
XLA Ops:
  0.0 18.8 %shard_map.55 = bf16[32,4096]{1,0:T(8,128)(2,1)S(1)} custom-call(bf16[32,4096]{1,0:T(8,128)(2,1)} %tok_hbm.1, s32[8,32]{1,0:T(8,128)} %bitcast.2, bf16[8,32]{1,0:T(8,128)(2,1)} %bitcast.3, bf16[1,4096,768]{2,1,0:T(8,128)(2,1)} %win_hbm.1, bf16[1,384,4096]{2,1,0:T(8,128)(2,1)} %wout_hbm.1), custom_call_target="tpu_custom_call" | custom-call | tf_op jit(solution)/shard_map/pallas_call | solution.py:255
  18.8 0.7 %copy.7 = bf16[32,4096]{1,0:T(8,128)(2,1)} copy(bf16[32,4096]{1,0:T(8,128)(2,1)S(1)} %shard_map.55) | data formatting | bytes 524288

commit v15 on v14

--- a/solution.py
+++ b/solution.py
@@ -11,7 +11,7 @@
 PACK = 2 * SRC_CAP
 IN_CHUNKS = 4
 OUT_CHUNKS = 2
-RELAY_IN = 2
+RELAY_IN = 3
 MESH = pl.DeviceIdType.MESH
 
 

time: 19.7 us -> 21 us (1.066)
  Pallas kernels: 18.8 us -> 20.1 us
    pallas_call x1, Pallas kernels: 18.8 us -> 20.1 us  [body(): pl.pallas_call(partial(kernel, n), out_shape=pltpu.VMEM((local, width), d...]
where the time goes in v15:
time: 21 us; the launch traced here: 20.8 us
  Pallas kernels  20.1 us (96%)
  local copies, waits for them, and re-layouts  0.71 us (3%)
    pallas_call x1, Pallas kernels, body(): pl.pallas_call(partial(kernel, n), out_shape=pltpu.VMEM((local, width), d...  20.1 us
    unnamed x1, local copies, waits for them, and re-layouts  0.71 us

profile of v15, /device:TPU:0, one launch (start us, length us, event | category | flops | bytes accessed | tf_op | source)
XLA Modules:
  0.0 20.8 jit_solution(11188805571854271658)
XLA Ops:
  0.0 20.1 %shard_map.55 = bf16[32,4096]{1,0:T(8,128)(2,1)S(1)} custom-call(bf16[32,4096]{1,0:T(8,128)(2,1)} %tok_hbm.1, s32[8,32]{1,0:T(8,128)} %bitcast.2, bf16[8,32]{1,0:T(8,128)(2,1)} %bitcast.3, bf16[1,4096,768]{2,1,0:T(8,128)(2,1)} %win_hbm.1, bf16[1,384,4096]{2,1,0:T(8,128)(2,1)} %wout_hbm.1), custom_call_target="tpu_custom_call" | custom-call | tf_op jit(solution)/shard_map/pallas_call | solution.py:255
  20.1 0.7 %copy.7 = bf16[32,4096]{1,0:T(8,128)(2,1)} copy(bf16[32,4096]{1,0:T(8,128)(2,1)S(1)} %shard_map.55) | data formatting | bytes 524288
